TPU v7x, 512 devices: a whole 4x8x8 slice. The times are simulated.
512 devices in a mesh: context: 32 (over z, y_lo), tensor: 8 (over x, y_hi), section: 2 (over core).
Axes of the slice: x: 4, y: 8 (y_hi: 2, y_lo: 4; y = y_hi * 4 + y_lo), z: 8, core: 2. Of those that a mesh axis runs over, the one named last changes fastest.
Arguments:
- queries: bfloat16 [2, 8192, 4096], P('section', 'context', 'tensor'), may hold values from -6 to 6
- keys: bfloat16 [2, 8192, 4096], P('section', 'context', 'tensor'), may hold values from -6 to 6
- values: bfloat16 [2, 8192, 4096], P('section', 'context', 'tensor'), may hold values from -6 to 6
- short_filters: float32 [2, 3, 3, 4096], P('section', None, None, 'tensor'), may hold values from -3 to 3
- decay_rates: float32 [2, 16, 4096], P('section', None, 'tensor'), may hold values from 3.0517578e-05 to 0.05
- residues: float32 [2, 16, 4096], P('section', None, 'tensor'), may hold values from -0.078125 to 0.078125
- out_weight: bfloat16 [2, 4096, 4096], P('section', 'tensor', 'context'), may hold values from -0.09375 to 0.09375
- rotation_signs: int32 [2, 4096], P('section', 'tensor'), may hold values from 0 to 1
Outputs:
- passed: bfloat16 [2, 8192, 4096], P('section', 'context', 'tensor')
All inputs are finite; a program needn't handle non-finite values.
Results may differ from a plain program's by a relative error of at most 0.0065.
Values may be sent and summed in bfloat16 or wider, within the bound.
No kernel may reach another device: no remote copies, remote signals or barrier semaphores. Data moves between devices by JAX's collectives and lax.ppermute only.
A program may use at most 64 MiB of HBM per device.

v0:
```python
import math

import jax
import jax.numpy as jnp
import numpy as np
from jax import lax
from jax.experimental import pallas as pl
from jax.experimental.pallas import tpu as pltpu
from jax.sharding import PartitionSpec as P

HB = 512
Z = 8
YL = 4
TENSOR = 8
TAPS = 3
MODES = 16
LANES = 128
SUBS = 8
PACKET = 32

f32 = jnp.float32
bf16 = jnp.bfloat16


def sylvester(order):
    index = np.arange(order)
    both = index[:, None] & index[None, :]
    bits = np.zeros_like(both)
    while both.any():
        bits += both & 1
        both = both >> 1
    return np.where(bits % 2 == 0, 1.0, -1.0).astype(np.float32)


def place():
    context = lax.axis_index("context")
    return context // YL, context % YL


def rounded(value):
    return value.astype(bf16).astype(f32)


def spread_kernel(q_ref, k_ref, v_ref, out_ref):
    for stream, ref in enumerate((q_ref, k_ref, v_ref)):
        for part in range(YL):
            out_ref[part, stream] = ref[0, :, part * LANES : (part + 1) * LANES]


def states_kernel(place, in_ref, filter_ref, decay_ref, mixed_ref, query_ref, before_ref, packet_ref, padded, ends):
    rows = mixed_ref.shape[0]
    part = in_ref.shape[2]
    step = rows // SUBS
    _, y_lo = place()
    lanes = pl.ds(pl.multiple_of(y_lo * LANES, LANES), LANES)
    features = []
    for stream in range(3):
        padded[0:8, :] = jnp.zeros((8, LANES), f32)
        for source in range(in_ref.shape[0]):
            padded[8 + source * part : 8 + (source + 1) * part, :] = in_ref[source, stream].astype(f32)
        taps = [filter_ref[0, stream, i : i + 1, lanes] for i in range(TAPS)]
        feature = taps[0] * padded[8 : 8 + rows, :]
        feature = feature + taps[1] * padded[7 : 7 + rows, :]
        feature = feature + taps[2] * padded[6 : 6 + rows, :]
        last = padded[6 + rows : 8 + rows, :]
        first = padded[8:10, :]
        features.append((first, last))
        if stream == 0:
            query_ref[...] = feature
        elif stream == 1:
            mixed_ref[...] = feature
        else:
            mixed_ref[...] = rounded(mixed_ref[...] * feature)
    mixed_ref[0:2, :] = jnp.zeros((2, LANES), f32)

    decay = decay_ref[0, :, lanes]
    factor = jnp.exp(-decay)
    factors = [jnp.broadcast_to(factor[m : m + 1, :], (SUBS, LANES)) for m in range(MODES)]

    def advance(i, state):
        x = mixed_ref[pl.ds(i, SUBS, stride=step), :]
        return tuple(a * h + x for a, h in zip(factors, state))

    state = lax.fori_loop(0, step, advance, tuple(jnp.zeros((SUBS, LANES), f32) for _ in range(MODES)), unroll=4)
    for m in range(MODES):
        ends[m] = state[m]
    over = jnp.exp(-decay * step)
    total = jnp.zeros((MODES, LANES), f32)
    for s in range(SUBS):
        before_ref[:, s, :] = total
        total = over * total + ends[:, s, :]
    edges = jnp.concatenate(
        [
            features[1][0],
            features[2][0],
            features[1][1],
            features[2][1],
            features[0][1],
            jnp.zeros((PACKET - MODES - 10, LANES), f32),
        ],
        axis=0,
    )
    for target in range(packet_ref.shape[0]):
        packet_ref[target, 0:MODES, :] = total
        packet_ref[target, MODES:PACKET, :] = edges


def gate_kernel(place, packet_ref, mixed_ref, query_ref, before_ref, filter_ref, decay_ref, residue_ref, out_ref, gated):
    rows = mixed_ref.shape[0]
    step = rows // SUBS
    z, y_lo = place()
    lanes = pl.ds(pl.multiple_of(y_lo * LANES, LANES), LANES)
    taps = [[filter_ref[0, stream, i : i + 1, lanes] for i in range(TAPS)] for stream in range(3)]
    decay = decay_ref[0, :, lanes]

    def first_rows(own, behind, there):
        def row(ref, at):
            return ref[MODES + at : MODES + at + 1, :]

        def last(at):
            return jnp.where(there, row(behind, at), 0.0)

        def pair(stream, start, end):
            w = taps[stream]
            zero = w[0] * row(own, start) + w[1] * last(end + 1) + w[2] * last(end)
            one = w[0] * row(own, start + 1) + w[1] * row(own, start) + w[2] * last(end + 1)
            return zero, one

        key = pair(1, 0, 4)
        value = pair(2, 2, 6)
        return [rounded(a * b) for a, b in zip(key, value)]

    carry = jnp.zeros((MODES, LANES), f32)
    far = jnp.exp(-decay * rows)
    near0 = jnp.exp(-decay * (rows - 1))
    near1 = jnp.exp(-decay * (rows - 2))
    for plane in range(Z - 1):
        x0, x1 = first_rows(packet_ref.at[plane], packet_ref.at[max(plane - 1, 0)], plane > 0)
        total = packet_ref[plane, 0:MODES, :] + near0 * x0 + near1 * x1
        carry = jnp.where(plane < z, far * carry + total, carry)
    behind = packet_ref.at[jnp.maximum(z - 1, 0)]
    x0, x1 = first_rows(packet_ref.at[z], behind, z > 0)
    q2 = jnp.where(z > 0, behind[MODES + 8 : MODES + 9, :], 0.0)
    q1 = jnp.where(z > 0, behind[MODES + 9 : MODES + 10, :], 0.0)

    sub = lax.broadcasted_iota(jnp.int32, (SUBS, LANES), 0)
    head = sub == 0
    start = (sub * step).astype(f32)
    factor = jnp.exp(-decay)
    residue = residue_ref[0, :, lanes]
    factors, weights, state = [], [], []
    for m in range(MODES):
        factors.append(jnp.broadcast_to(factor[m : m + 1, :], (SUBS, LANES)))
        weights.append(jnp.broadcast_to(residue[m : m + 1, :], (SUBS, LANES)))
        rate = decay[m : m + 1, :]
        entered = before_ref[m] + jnp.exp(-rate * start) * carry[m : m + 1, :]
        edge = jnp.exp(-rate * (start - 1.0)) * x0 + jnp.exp(-rate * (start - 2.0)) * x1
        state.append(entered + jnp.where(head, 0.0, edge))

    def advance(i, state, x, query):
        state = tuple(a * h + x for a, h in zip(factors, state))
        terms = [w * h for w, h in zip(weights, state)]
        while len(terms) > 1:
            terms = [a + b for a, b in zip(terms[::2], terms[1::2])]
        gated[pl.ds(i, SUBS, stride=step), :] = query * rounded(terms[0])
        return state

    def load(ref, i):
        return ref[pl.ds(i, SUBS, stride=step), :]

    w = taps[0]
    state = tuple(state)
    query = load(query_ref, 0)
    query = jnp.where(head, (query + w[1] * q1) + w[2] * q2, query)
    state = advance(0, state, load(mixed_ref, 0) + jnp.where(head, x0, 0.0), query)
    query = load(query_ref, 1)
    query = jnp.where(head, query + w[2] * q1, query)
    state = advance(1, state, load(mixed_ref, 1) + jnp.where(head, x1, 0.0), query)
    lax.fori_loop(
        2, step, lambda i, state: advance(i, state, load(mixed_ref, i), load(query_ref, i)), state, unroll=2
    )
    result = gated[...].astype(bf16)
    for target in range(out_ref.shape[0]):
        out_ref[target] = result


def product_kernel(a_ref, w_ref, out_ref):
    rows = jnp.concatenate([a_ref[i] for i in range(YL)], axis=1)
    for pair in range(Z // 2):
        weight = jnp.concatenate([w_ref[2 * pair], w_ref[2 * pair + 1]], axis=1)
        result = jnp.dot(rows, weight, preferred_element_type=f32).astype(bf16)
        out_ref[2 * pair] = result[:, :LANES]
        out_ref[2 * pair + 1] = result[:, LANES:]


def rotate_kernel(in_ref, sign_ref, matrix_ref, out_ref):
    columns = []
    for part in range(YL):
        total = in_ref[part * TENSOR].astype(f32)
        for source in range(1, TENSOR):
            total = total + in_ref[part * TENSOR + source].astype(f32)
        columns.append(total)
    sign = (2 * sign_ref[...] - 1).astype(f32)
    signed = jnp.concatenate(columns, axis=1) * sign
    high = signed.astype(bf16)
    rest = signed - high.astype(f32)
    middle = rest.astype(bf16)
    low = (rest - middle.astype(f32)).astype(bf16)
    matrix = matrix_ref[...]
    turned = jnp.dot(low, matrix, preferred_element_type=f32)
    turned = turned + jnp.dot(middle, matrix, preferred_element_type=f32)
    turned = turned + jnp.dot(high, matrix, preferred_element_type=f32)
    out_ref[...] = (turned * (1.0 / math.sqrt(HB))).astype(bf16)


PARAMS = pltpu.CompilerParams(vmem_limit_bytes=32 * 1024 * 1024)


def spread(q, k, v):
    rows, width = q.shape[1:]
    return pl.pallas_call(
        spread_kernel,
        out_shape=jax.ShapeDtypeStruct((YL, 3, rows, width // YL), bf16),
        compiler_params=PARAMS,
        name="spread",
    )(q, k, v)


def states(arrived, filters, decay, place=place):
    rows = arrived.shape[0] * arrived.shape[2]
    return pl.pallas_call(
        lambda *refs: states_kernel(place, *refs),
        out_shape=(
            jax.ShapeDtypeStruct((rows, LANES), f32),
            jax.ShapeDtypeStruct((rows, LANES), f32),
            jax.ShapeDtypeStruct((MODES, SUBS, LANES), f32),
            jax.ShapeDtypeStruct((Z, PACKET, LANES), f32),
        ),
        scratch_shapes=[pltpu.VMEM((rows + 8, LANES), f32), pltpu.VMEM((MODES, SUBS, LANES), f32)],
        compiler_params=PARAMS,
        name="states",
    )(arrived, filters, decay)


def gate(packets, mixed, query, before, filters, decay, residues, place=place):
    rows = mixed.shape[0]
    return pl.pallas_call(
        lambda *refs: gate_kernel(place, *refs),
        out_shape=jax.ShapeDtypeStruct((YL, rows, LANES), bf16),
        scratch_shapes=[pltpu.VMEM((rows, LANES), f32)],
        compiler_params=PARAMS,
        name="gate",
    )(packets, mixed, query, before, filters, decay, residues)


def product(gated, weight):
    rows = gated.shape[1] // YL
    return pl.pallas_call(
        product_kernel,
        grid=(YL,),
        in_specs=[
            pl.BlockSpec((YL, rows, LANES), lambda i: (0, i, 0)),
            pl.BlockSpec(weight.shape, lambda i: (0, 0, 0)),
        ],
        out_specs=pl.BlockSpec((Z, rows, LANES), lambda i: (i, 0, 0)),
        out_shape=jax.ShapeDtypeStruct((YL * Z, rows, LANES), bf16),
        compiler_params=PARAMS,
        name="product",
    )(gated, weight)


def rotate(partials, signs, matrix):
    sources, rows, _ = partials.shape
    chunk = 64
    return pl.pallas_call(
        rotate_kernel,
        grid=(rows // chunk,),
        in_specs=[
            pl.BlockSpec((sources, chunk, LANES), lambda i: (0, i, 0)),
            pl.BlockSpec(signs.shape, lambda i: (0, 0)),
            pl.BlockSpec(matrix.shape, lambda i: (0, 0)),
        ],
        out_specs=pl.BlockSpec((chunk, HB), lambda i: (i, 0)),
        out_shape=jax.ShapeDtypeStruct((rows, HB), bf16),
        compiler_params=PARAMS,
        name="rotate",
    )(partials, signs, matrix)


Y_GROUPS = [[z * YL + y for y in range(YL)] for z in range(Z)]
Z_GROUPS = [[z * YL + y for z in range(Z)] for y in range(YL)]
PLANES = [[(z * YL + y) * TENSOR + t for y in range(YL) for t in range(TENSOR)] for z in range(Z)]


def shards(queries, keys, values, short_filters, decay_rates, residues, out_weight, rotation_signs):
    weight = lax.all_gather(out_weight[0], "context", axis=0, axis_index_groups=Z_GROUPS)
    sent = spread(queries, keys, values)
    arrived = lax.all_to_all(sent, "context", 0, 0, axis_index_groups=Y_GROUPS)
    mixed, query, before, packets = states(arrived, short_filters, decay_rates)
    packets = lax.all_to_all(packets, "context", 0, 0, axis_index_groups=Z_GROUPS)
    gated = gate(packets, mixed, query, before, short_filters, decay_rates, residues)
    gated = lax.all_to_all(gated, "context", 0, 0, axis_index_groups=Y_GROUPS)
    partials = product(gated, weight)
    partials = lax.all_to_all(partials, ("context", "tensor"), 0, 0, axis_index_groups=PLANES)
    rotated = rotate(partials, rotation_signs, jnp.asarray(sylvester(HB), bf16))
    handed = lax.ppermute(rotated, "section", [(0, 1), (1, 0)])
    return handed[None]


def solution(mesh):
    in_specs = (
        P("section", "context", "tensor"),
        P("section", "context", "tensor"),
        P("section", "context", "tensor"),
        P("section", None, None, "tensor"),
        P("section", None, "tensor"),
        P("section", None, "tensor"),
        P("section", "tensor", "context"),
        P("section", "tensor"),
    )
    out_specs = P("section", "context", "tensor")
    return jax.shard_map(shards, mesh=mesh, in_specs=in_specs, out_specs=out_specs, check_vma=False)
```

profile of v0, /device:TPU:9, one launch (start us, length us, event | category | flops | bytes accessed | tf_op | source)
XLA Modules:
  0.0 163.6 jit_solution(2873880687696510795)
XLA Ops:
  6.5 0.0 copy-start.2
  6.5 0.9 copy-done.2
  7.5 0.0 copy-start.3
  7.5 0.9 copy-done.3
  8.4 0.0 copy-start.4
  8.4 0.9 copy-done.4
  9.4 0.0 copy-start.8
  9.4 0.0 copy-start.5
  9.4 0.0 copy-start.6
  9.4 1.1 spread.1
  10.5 4.8 %all-to-all-start = ((bf16[4,3,256,128]{3,2,1,0:T(8,128)(2,1)}), bf16[4,3,256,128]{3,2,1,0:T(8,128)(2,1)S(1)}, u32[]{:S(2)}, u32[]{:S(2)}) async-start(bf16[4,3,256,128]{3,2,1,0:T(8,128)(2,1)} %spread.1), calls=%async_computation | async-start | bytes 1572864 | tf_op jit(solution)/shard_map/all_to_all | solution.py:298
  15.2 0.0 all-gather.2.cloned.1.call-start
  15.2 0.7 all-gather.2.cloned.1.call-update
  15.9 0.0 copy-done.8
  16.0 14.8 %all-to-all-done.refs_0_ = bf16[4,3,256,128]{3,2,1,0:T(8,128)(2,1)S(1)} async-done(((bf16[4,3,256,128]{3,2,1,0:T(8,128)(2,1)}), bf16[4,3,256,128]{3,2,1,0:T(8,128)(2,1)S(1)}, u32[]{:S(2)}, u32[]{:S(2)}) %all-to-all-start) | async-done | bytes 786464 | tf_op jit(solution)/shard_map/all_to_all | solution.py:298
  30.7 0.0 copy-done.5
  30.7 1.8 %states.1 = (f32[1024,128]{1,0:T(8,128)S(1)}, f32[1024,128]{1,0:T(8,128)S(1)}, f32[16,8,128]{2,1,0:T(8,128)S(1)}, f32[8,32,128]{2,1,0:T(8,128)S(1)}) custom-call(bf16[4,3,256,128]{3,2,1,0:T(8,128)(2,1)S(1)} %all-to-all-done.refs_0_, f32[1,3,3,512]{3,2,1,0:T(4,128)S(1)} %copy.12.refs_1_.refs_4_, f32[1,16,512]{2,1,0:T(8,128)S(1)} %copy-done.5), custom_call_target="tpu_custom_call" | custom-call | tf_op jit(solution)/shard_map/states/pallas_call | solution.py:231
  32.5 19.6 %all_to_all.20.refs_0_ = f32[8,32,128]{2,1,0:T(8,128)S(1)} all-to-all(f32[8,32,128]{2,1,0:T(8,128)S(1)} %get-tuple-element.9), channel_id=1, replica_groups={{0,64,128,192,256,320,384,448},{16,80,144,208,272,336,400,464},{32,96,1..., dimensions={0} | all-to-all | bytes 262144 | tf_op jit(solution)/shard_map/all_to_all | solution.py:300
  52.1 0.0 copy-done.6
  52.1 3.5 %gate.1 = bf16[4,1024,128]{2,1,0:T(8,128)(2,1)} custom-call(f32[8,32,128]{2,1,0:T(8,128)S(1)} %all_to_all.20.refs_0_, f32[1024,128]{1,0:T(8,128)S(1)} %get-tuple-element.10.refs_1_, f32[1024,128]{1,0:T(8,128)S(1)} %get-tuple-element.11.refs_2_, f32[16,8,128]{2,1,0:T(8,128)S(1)} %get-tuple-element.12.refs_3_, f32[1,3,3,512]{3,2,1,0:T(4,128)S(1)} %copy.12.refs_1_.refs_4_, ...), custom_call_target="tpu_custom_call" | custom-call | tf_op jit(solution)/shard_map/gate/pallas_call | solution.py:247
  55.6 7.4 %all-to-all-start.2 = ((bf16[4,1024,128]{2,1,0:T(8,128)(2,1)}), bf16[4,1024,128]{2,1,0:T(8,128)(2,1)S(1)}, u32[]{:S(2)}, u32[]{:S(2)}) async-start(bf16[4,1024,128]{2,1,0:T(8,128)(2,1)} %gate.1), calls=%async_computation.2 | async-start | bytes 2097152 | tf_op jit(solution)/shard_map/all_to_all | solution.py:302
  63.1 0.0 all-gather.2.cloned.1.call-done.w_ref
  63.1 20.5 %all-to-all-done.2.a_ref = bf16[4,1024,128]{2,1,0:T(8,128)(2,1)S(1)} async-done(((bf16[4,1024,128]{2,1,0:T(8,128)(2,1)}), bf16[4,1024,128]{2,1,0:T(8,128)(2,1)S(1)}, u32[]{:S(2)}, u32[]{:S(2)}) %all-to-all-start.2) | async-done | bytes 1048608 | tf_op jit(solution)/shard_map/all_to_all | solution.py:302
  83.5 0.0 copy-start
  83.5 1.2 copy-done
  84.8 1.9 %product.1 = bf16[32,256,128]{2,1,0:T(8,128)(2,1)S(1)} custom-call(bf16[4,1024,128]{2,1,0:T(8,128)(2,1)S(1)} %all-to-all-done.2.a_ref, bf16[8,512,128]{2,1,0:T(8,128)(2,1)S(1)} %copy-done), custom_call_target="tpu_custom_call" | custom-call | tf_op jit(solution)/shard_map/product/pallas_call | solution.py:258
  86.7 0.0 copy-start.1
  86.7 0.0 copy-start.7
  86.7 63.0 %all_to_all.21.in_ref = bf16[32,256,128]{2,1,0:T(8,128)(2,1)S(1)} all-to-all(bf16[32,256,128]{2,1,0:T(8,128)(2,1)S(1)} %product.1), channel_id=1, replica_groups={{0,2,4,6,8,10,12,14,16,18,20,22,24,26,28,30,32,34,36,38,40,42,44,46,48,..., dimensions={0} | all-to-all | bytes 4194304 | tf_op jit(solution)/shard_map/all_to_all | solution.py:304
  149.7 0.0 copy-done.1
  149.7 0.0 copy-done.7
  149.7 1.7 %rotate.1 = bf16[256,512]{1,0:T(8,128)(2,1)S(1)} custom-call(bf16[32,256,128]{2,1,0:T(8,128)(2,1)S(1)} %all_to_all.21.in_ref, s32[1,512]{1,0:T(1,128)S(1)} %copy-done.7, bf16[512,512]{1,0:T(8,128)(2,1)S(1)} %copy-done.1), custom_call_target="tpu_custom_call" | custom-call | tf_op jit(solution)/shard_map/rotate/pallas_call | solution.py:275
  151.4 3.5 %collective-permute-start = (bf16[256,512]{1,0:T(8,128)(2,1)S(1)}, bf16[256,512]{1,0:T(8,128)(2,1)S(1)}, u32[]{:S(2)}, u32[]{:S(2)}) collective-permute-start(bf16[256,512]{1,0:T(8,128)(2,1)S(1)} %rotate.1), channel_id=1, source_target_pairs={{0,1},{1,0},{2,3},{3,2},{4,5},{5,4},{6,7},{7,6},{8,9},{9,8},{10,11... | collective-permute-start | bytes 786440 | tf_op jit(solution)/shard_map/ppermute | solution.py:306
  155.0 1.1 collective-permute-done
  156.1 0.7 copy.15
  (1 shorter events, 0.0 us)
Async XLA Ops:
  6.5 0.9 copy-start.2
  7.5 0.9 copy-start.3
  8.4 0.9 copy-start.4
  9.4 6.6 %copy-start.8 = (f32[1,3,3,512]{3,0,2,1:T(1,128)S(1)}, f32[1,3,3,512]{3,0,2,1:T(1,128)}, u32[]{:S(2)}) copy-start(f32[1,3,3,512]{3,0,2,1:T(1,128)} %param.12) | copy-start | bytes 55300
  9.4 21.3 %copy-start.5 = (f32[1,16,512]{2,1,0:T(8,128)S(1)}, f32[1,16,512]{2,1,0:T(8,128)}, u32[]{:S(2)}) copy-start(f32[1,16,512]{2,1,0:T(8,128)} %refs_5_.1) | copy-start | bytes 98308
  9.4 42.7 %copy-start.6 = (f32[1,16,512]{2,1,0:T(8,128)S(1)}, f32[1,16,512]{2,1,0:T(8,128)}, u32[]{:S(2)}) copy-start(f32[1,16,512]{2,1,0:T(8,128)} %refs_6_.1) | copy-start | bytes 98308
  10.5 20.3 %all-to-all-start = ((bf16[4,3,256,128]{3,2,1,0:T(8,128)(2,1)}), bf16[4,3,256,128]{3,2,1,0:T(8,128)(2,1)S(1)}, u32[]{:S(2)}, u32[]{:S(2)}) async-start(bf16[4,3,256,128]{3,2,1,0:T(8,128)(2,1)} %spread.1), calls=%async_computation | async-start | bytes 1572864 | tf_op jit(solution)/shard_map/all_to_all | solution.py:298
  15.2 47.9 %all-gather.2.cloned.1.call-start = ((), (), s32[]{:S(2)}) async-start(), calls=%async_computation.4 | async-start | bytes 1179648 | tf_op jit(solution)/shard_map/all_gather | solution.py:296
  55.6 27.9 %all-to-all-start.2 = ((bf16[4,1024,128]{2,1,0:T(8,128)(2,1)}), bf16[4,1024,128]{2,1,0:T(8,128)(2,1)S(1)}, u32[]{:S(2)}, u32[]{:S(2)}) async-start(bf16[4,1024,128]{2,1,0:T(8,128)(2,1)} %gate.1), calls=%async_computation.2 | async-start | bytes 2097152 | tf_op jit(solution)/shard_map/all_to_all | solution.py:302
  83.5 1.2 copy-start
  86.7 63.1 %copy-start.1 = (bf16[512,512]{1,0:T(8,128)(2,1)S(1)}, bf16[512,512]{1,0:T(8,128)(2,1)}, u32[]{:S(2)}) copy-start(bf16[512,512]{1,0:T(8,128)(2,1)} %constant.2.clone.matrix_ref) | copy-start | bytes 1572868
  86.7 63.0 %copy-start.7 = (s32[1,512]{1,0:T(1,128)S(1)}, s32[1,512]{1,0:T(1,128)}, u32[]{:S(2)}) copy-start(s32[1,512]{1,0:T(1,128)} %sign_ref.1) | copy-start | bytes 6148
  151.4 4.7 %collective-permute-start = (bf16[256,512]{1,0:T(8,128)(2,1)S(1)}, bf16[256,512]{1,0:T(8,128)(2,1)S(1)}, u32[]{:S(2)}, u32[]{:S(2)}) collective-permute-start(bf16[256,512]{1,0:T(8,128)(2,1)S(1)} %rotate.1), channel_id=1, source_target_pairs={{0,1},{1,0},{2,3},{3,2},{4,5},{5,4},{6,7},{7,6},{8,9},{9,8},{10,11... | collective-permute-start | bytes 786440 | tf_op jit(solution)/shard_map/ppermute | solution.py:306
Sparse Core Ops, SparseCore 0:
  18.1 41.7 all-gather.1
where the time goes:
time: 164 us
  blocking collectives  82.6 us (50%)
  waiting for transfers between devices  37.1 us (23%)
  starting transfers between devices  15.7 us (10%)
  between operations  13.5 us (8%)
  Pallas kernels  9.94 us (6%)
  local copies, waits for them, and re-layouts  4.81 us (3%)
    all_to_all x1, blocking collectives, shards(): lax.all_to_all(partials, ('context', 'tensor'), 0, 0, axis_index_groups=P...  63 us
    all_to_all x1, waiting for transfers between devices, shards(): gated = lax.all_to_all(gated, 'context', 0, 0, axis_index_groups=Y_GROUPS)  20.5 us
    all_to_all x1, blocking collectives, shards(): lax.all_to_all(packets, 'context', 0, 0, axis_index_groups=Z_GROUPS)  19.6 us
    all_to_all x1, waiting for transfers between devices, shards(): arrived = lax.all_to_all(sent, 'context', 0, 0, axis_index_groups=Y_GROUPS)  14.8 us
    all_to_all x1, starting transfers between devices, shards(): gated = lax.all_to_all(gated, 'context', 0, 0, axis_index_groups=Y_GROUPS)  7.43 us
    unnamed x20, local copies, waits for them, and re-layouts  4.81 us
    all_to_all x1, starting transfers between devices, shards(): arrived = lax.all_to_all(sent, 'context', 0, 0, axis_index_groups=Y_GROUPS)  4.76 us
    pallas_call x1, Pallas kernels, gate(): pl.pallas_call(lambda *refs: gate_kernel(place, *refs), out_shape=jax.Sha...  3.54 us
  transfers between devices with their start and end apart: 4, of which 3 were waited for; matrix products, arithmetic and copies ran while one was open for 0% of the time, Pallas kernels for 3%

commit v1 on v0

--- a/solution.py
+++ b/solution.py
@@ -11,7 +11,9 @@
 HB = 512
 Z = 8
 YL = 4
-TENSOR = 8
+X = 4
+YH = 2
+TENSOR = X * YH
 TAPS = 3
 MODES = 16
 LANES = 128
@@ -41,10 +43,16 @@
     return value.astype(bf16).astype(f32)
 
 
-def spread_kernel(q_ref, k_ref, v_ref, out_ref):
+def spread_kernel(q_ref, k_ref, v_ref, out_ref, sems):
+    copies = []
     for stream, ref in enumerate((q_ref, k_ref, v_ref)):
         for part in range(YL):
-            out_ref[part, stream] = ref[0, :, part * LANES : (part + 1) * LANES]
+            source = ref.at[0, :, part * LANES : (part + 1) * LANES]
+            copies.append(pltpu.make_async_copy(source, out_ref.at[part, stream], sems.at[stream * YL + part]))
+    for copy in copies:
+        copy.start()
+    for copy in copies:
+        copy.wait()
 
 
 def states_kernel(place, in_ref, filter_ref, decay_ref, mixed_ref, query_ref, before_ref, packet_ref, padded, ends):
@@ -179,27 +187,33 @@
     lax.fori_loop(
         2, step, lambda i, state: advance(i, state, load(mixed_ref, i), load(query_ref, i)), state, unroll=2
     )
-    result = gated[...].astype(bf16)
-    for target in range(out_ref.shape[0]):
-        out_ref[target] = result
-
-
-def product_kernel(a_ref, w_ref, out_ref):
-    rows = jnp.concatenate([a_ref[i] for i in range(YL)], axis=1)
-    for pair in range(Z // 2):
-        weight = jnp.concatenate([w_ref[2 * pair], w_ref[2 * pair + 1]], axis=1)
-        result = jnp.dot(rows, weight, preferred_element_type=f32).astype(bf16)
-        out_ref[2 * pair] = result[:, :LANES]
-        out_ref[2 * pair + 1] = result[:, LANES:]
+    half = rows // 2
+    for target in range(YH * YL):
+        start = target % YL // 2 * half
+        out_ref[target] = gated[start : start + half, :].astype(bf16)
+
+
+def product_kernel(place, a_ref, w_ref, out_ref):
+    _, y_lo = place()
+    group = y_lo // 2
+    rows = jnp.concatenate([a_ref[i] for i in range(YH * YL)], axis=1)
+    for x in range(X):
+        tiles = []
+        for c in range(2):
+            index = lax.rem(group + c, 2)
+            tiles.append(jnp.concatenate([w_ref[YH * x + r, index] for r in range(YH)], axis=0))
+        weight = jnp.concatenate(tiles, axis=1)
+        out_ref[x, 0] = jnp.dot(rows, weight, preferred_element_type=f32).astype(bf16)
 
 
 def rotate_kernel(in_ref, sign_ref, matrix_ref, out_ref):
-    columns = []
-    for part in range(YL):
-        total = in_ref[part * TENSOR].astype(f32)
-        for source in range(1, TENSOR):
-            total = total + in_ref[part * TENSOR + source].astype(f32)
-        columns.append(total)
+    sums = []
+    for b in range(2):
+        total = in_ref[b].astype(f32)
+        for x in range(1, X):
+            total = total + in_ref[2 * x + b].astype(f32)
+        sums.append(total)
+    columns = [sums[b][:, c * LANES : (c + 1) * LANES] for c in range(2) for b in range(2)]
     sign = (2 * sign_ref[...] - 1).astype(f32)
     signed = jnp.concatenate(columns, axis=1) * sign
     high = signed.astype(bf16)
@@ -220,7 +234,10 @@
     rows, width = q.shape[1:]
     return pl.pallas_call(
         spread_kernel,
+        in_specs=[pl.BlockSpec(memory_space=pltpu.HBM)] * 3,
+        out_specs=pl.BlockSpec(memory_space=pltpu.VMEM),
         out_shape=jax.ShapeDtypeStruct((YL, 3, rows, width // YL), bf16),
+        scratch_shapes=[pltpu.SemaphoreType.DMA((3 * YL,))],
         compiler_params=PARAMS,
         name="spread",
     )(q, k, v)
@@ -246,37 +263,38 @@
     rows = mixed.shape[0]
     return pl.pallas_call(
         lambda *refs: gate_kernel(place, *refs),
-        out_shape=jax.ShapeDtypeStruct((YL, rows, LANES), bf16),
+        out_shape=jax.ShapeDtypeStruct((YH * YL, rows // 2, LANES), bf16),
         scratch_shapes=[pltpu.VMEM((rows, LANES), f32)],
         compiler_params=PARAMS,
         name="gate",
     )(packets, mixed, query, before, filters, decay, residues)
 
 
-def product(gated, weight):
-    rows = gated.shape[1] // YL
-    return pl.pallas_call(
-        product_kernel,
-        grid=(YL,),
+def product(gated, weight, place=place):
+    sources, rows, _ = gated.shape
+    half = rows // 2
+    return pl.pallas_call(
+        lambda *refs: product_kernel(place, *refs),
+        grid=(2,),
         in_specs=[
-            pl.BlockSpec((YL, rows, LANES), lambda i: (0, i, 0)),
-            pl.BlockSpec(weight.shape, lambda i: (0, 0, 0)),
+            pl.BlockSpec((sources, half, LANES), lambda i: (0, i, 0)),
+            pl.BlockSpec(weight.shape, lambda i: (0, 0, 0, 0)),
         ],
-        out_specs=pl.BlockSpec((Z, rows, LANES), lambda i: (i, 0, 0)),
-        out_shape=jax.ShapeDtypeStruct((YL * Z, rows, LANES), bf16),
+        out_specs=pl.BlockSpec((X, 1, half, 2 * LANES), lambda i: (0, i, 0, 0)),
+        out_shape=jax.ShapeDtypeStruct((X, 2, half, 2 * LANES), bf16),
         compiler_params=PARAMS,
         name="product",
     )(gated, weight)
 
 
 def rotate(partials, signs, matrix):
-    sources, rows, _ = partials.shape
+    sources, rows, width = partials.shape
     chunk = 64
     return pl.pallas_call(
         rotate_kernel,
         grid=(rows // chunk,),
         in_specs=[
-            pl.BlockSpec((sources, chunk, LANES), lambda i: (0, i, 0)),
+            pl.BlockSpec((sources, chunk, width), lambda i: (0, i, 0)),
             pl.BlockSpec(signs.shape, lambda i: (0, 0)),
             pl.BlockSpec(matrix.shape, lambda i: (0, 0)),
         ],
@@ -287,21 +305,44 @@
     )(partials, signs, matrix)
 
 
+BOTH = ("context", "tensor")
+
+
+def at(z, yl, x, yh):
+    return (z * YL + yl) * TENSOR + x * YH + yh
+
+
 Y_GROUPS = [[z * YL + y for y in range(YL)] for z in range(Z)]
 Z_GROUPS = [[z * YL + y for z in range(Z)] for y in range(YL)]
-PLANES = [[(z * YL + y) * TENSOR + t for y in range(YL) for t in range(TENSOR)] for z in range(Z)]
+LINES = [[at(z, y, x, h) for h in range(YH) for y in range(YL)] for z in range(Z) for x in range(X)]
+SQUARES = [
+    [at(z, 2 * g + b, x, h) for x in range(X) for b in range(2)] for z in range(Z) for g in range(2) for h in range(YH)
+]
+
+
+def weight_route(turn):
+    route = []
+    for z in range(Z):
+        for y in range(YL):
+            for x in range(X):
+                for h in range(YH):
+                    target = (z - z % 2 + h, y ^ (2 * turn), x, z % 2)
+                    route.append((at(z, y, x, h), at(*target)))
+    return route
 
 
 def shards(queries, keys, values, short_filters, decay_rates, residues, out_weight, rotation_signs):
-    weight = lax.all_gather(out_weight[0], "context", axis=0, axis_index_groups=Z_GROUPS)
+    pieces = [lax.ppermute(out_weight[0], BOTH, weight_route(turn)) for turn in range(2)]
+    weight = lax.all_gather(jnp.stack(pieces), "context", axis=0, axis_index_groups=Z_GROUPS)
     sent = spread(queries, keys, values)
     arrived = lax.all_to_all(sent, "context", 0, 0, axis_index_groups=Y_GROUPS)
     mixed, query, before, packets = states(arrived, short_filters, decay_rates)
     packets = lax.all_to_all(packets, "context", 0, 0, axis_index_groups=Z_GROUPS)
     gated = gate(packets, mixed, query, before, short_filters, decay_rates, residues)
-    gated = lax.all_to_all(gated, "context", 0, 0, axis_index_groups=Y_GROUPS)
+    gated = lax.all_to_all(gated, BOTH, 0, 0, axis_index_groups=LINES)
     partials = product(gated, weight)
-    partials = lax.all_to_all(partials, ("context", "tensor"), 0, 0, axis_index_groups=PLANES)
+    rows = partials.shape[2]
+    partials = lax.all_to_all(partials.reshape(2 * X, rows, -1), BOTH, 0, 0, axis_index_groups=SQUARES)
     rotated = rotate(partials, rotation_signs, jnp.asarray(sylvester(HB), bf16))
     handed = lax.ppermute(rotated, "section", [(0, 1), (1, 0)])
     return handed[None]

time: 164 us -> 145 us (0.88)
  the two profiles are of different devices: /device:TPU:9 before, /device:TPU:1 now
where the time goes in v1:
time: 145 us
  blocking collectives  69.2 us (48%)
  waiting for transfers between devices  26.1 us (18%)
  starting transfers between devices  21.3 us (15%)
  between operations  13.5 us (9%)
  Pallas kernels  8.75 us (6%)
  local copies, waits for them, and re-layouts  5.17 us (4%)
    all_to_all x1, blocking collectives, shards(): gated = lax.all_to_all(gated, BOTH, 0, 0, axis_index_groups=LINES)  30.6 us
    all_to_all x1, blocking collectives, shards(): lax.all_to_all(packets, 'context', 0, 0, axis_index_groups=Z_GROUPS)  24.3 us
    all_to_all x1, waiting for transfers between devices, shards(): arrived = lax.all_to_all(sent, 'context', 0, 0, axis_index_groups=Y_GROUPS)  19.6 us
    all_to_all x1, blocking collectives, shards(): lax.all_to_all(partials.reshape(2 * X, rows, -1), BOTH, 0, 0, axis_index_...  14.3 us
    ppermute x1, starting transfers between devices, shards(): handed = lax.ppermute(rotated, 'section', [(0, 1), (1, 0)])  8.34 us
    ppermute x2, starting transfers between devices, shards(): lax.ppermute(out_weight[0], BOTH, weight_route(turn))  6.72 us
    all_to_all x1, starting transfers between devices, shards(): arrived = lax.all_to_all(sent, 'context', 0, 0, axis_index_groups=Y_GROUPS)  6.23 us
    ppermute x2, waiting for transfers between devices, shards(): lax.ppermute(out_weight[0], BOTH, weight_route(turn))  5.35 us
  transfers between devices with their start and end apart: 5, of which 3 were waited for; matrix products, arithmetic and copies ran while one was open for 0% of the time, Pallas kernels for 4%

profile of v1, /device:TPU:1, one launch (start us, length us, event | category | flops | bytes accessed | tf_op | source)
XLA Modules:
  0.0 144.7 jit_solution(6688394972308603162)
XLA Ops:
  6.5 0.0 copy-start.8
  6.5 0.0 copy-start.5
  6.5 0.0 all-gather.3.cloned.1.call-start
  6.5 1.7 %collective-permute-start = (bf16[512,128]{1,0:T(8,128)(2,1)}, bf16[512,128]{1,0:T(8,128)(2,1)S(1)}, u32[]{:S(2)}, u32[]{:S(2)}) collective-permute-start(bf16[512,128]{1,0:T(8,128)(2,1)} %bitcast.11), channel_id=1, source_target_pairs={{0,0},{2,64},{4,4},{6,68},{8,8},{10,72},{12,12},{14,76},{16,16},{1... | collective-permute-start | bytes 393224 | tf_op jit(solution)/shard_map/ppermute | solution.py:335
  8.2 5.0 %collective-permute-start.1 = (bf16[512,128]{1,0:T(8,128)(2,1)}, bf16[512,128]{1,0:T(8,128)(2,1)S(1)}, u32[]{:S(2)}, u32[]{:S(2)}) collective-permute-start(bf16[512,128]{1,0:T(8,128)(2,1)} %bitcast.12), channel_id=1, source_target_pairs={{0,32},{2,96},{4,36},{6,100},{8,40},{10,104},{12,44},{14,108},{16,... | collective-permute-start | bytes 393224 | tf_op jit(solution)/shard_map/ppermute | solution.py:335
  13.3 0.0 collective-permute-done
  13.3 5.4 %collective-permute-done.1 = bf16[512,128]{1,0:T(8,128)(2,1)S(1)} collective-permute-done((bf16[512,128]{1,0:T(8,128)(2,1)}, bf16[512,128]{1,0:T(8,128)(2,1)S(1)}, u32[]{:S(2)}, u32[]{:S(2)}) %collective-permute-start.1) | collective-permute-done | bytes 131104 | tf_op jit(solution)/shard_map/ppermute | solution.py:335
  18.6 0.7 pad_maximum_fusion
  19.4 0.0 all-gather.3.cloned.1.call-update
  19.4 0.0 copy-start.2
  19.4 0.9 copy-done.2
  20.3 0.0 copy-start.3
  20.3 0.9 copy-done.3
  21.3 0.0 copy-start.4
  21.3 0.9 copy-done.4
  22.2 0.0 copy-start.6
  22.2 1.2 spread.1
  23.4 6.2 %all-to-all-start = ((bf16[4,3,256,128]{3,2,1,0:T(8,128)(2,1)}), bf16[4,3,256,128]{3,2,1,0:T(8,128)(2,1)S(1)}, u32[]{:S(2)}, u32[]{:S(2)}) async-start(bf16[4,3,256,128]{3,2,1,0:T(8,128)(2,1)} %spread.1), calls=%async_computation | async-start | bytes 1572864 | tf_op jit(solution)/shard_map/all_to_all | solution.py:338
  29.6 0.0 copy-done.8
  29.6 19.6 %all-to-all-done.refs_0_ = bf16[4,3,256,128]{3,2,1,0:T(8,128)(2,1)S(1)} async-done(((bf16[4,3,256,128]{3,2,1,0:T(8,128)(2,1)}), bf16[4,3,256,128]{3,2,1,0:T(8,128)(2,1)S(1)}, u32[]{:S(2)}, u32[]{:S(2)}) %all-to-all-start) | async-done | bytes 786464 | tf_op jit(solution)/shard_map/all_to_all | solution.py:338
  49.2 0.0 copy-done.5
  49.2 1.8 %states.1 = (f32[1024,128]{1,0:T(8,128)S(1)}, f32[1024,128]{1,0:T(8,128)S(1)}, f32[16,8,128]{2,1,0:T(8,128)S(1)}, f32[8,32,128]{2,1,0:T(8,128)S(1)}) custom-call(bf16[4,3,256,128]{3,2,1,0:T(8,128)(2,1)S(1)} %all-to-all-done.refs_0_, f32[1,3,3,512]{3,2,1,0:T(4,128)S(1)} %copy.12.refs_1_.refs_4_, f32[1,16,512]{2,1,0:T(8,128)S(1)} %copy-done.5), custom_call_target="tpu_custom_call" | custom-call | tf_op jit(solution)/shard_map/states/pallas_call | solution.py:248
  51.0 24.3 %all_to_all.20.refs_0_ = f32[8,32,128]{2,1,0:T(8,128)S(1)} all-to-all(f32[8,32,128]{2,1,0:T(8,128)S(1)} %get-tuple-element.9), channel_id=1, replica_groups={{0,64,128,192,256,320,384,448},{16,80,144,208,272,336,400,464},{32,96,1..., dimensions={0} | all-to-all | bytes 262144 | tf_op jit(solution)/shard_map/all_to_all | solution.py:340
  75.3 0.0 copy-done.6
  75.3 2.5 %gate.1 = bf16[8,512,128]{2,1,0:T(8,128)(2,1)S(1)} custom-call(f32[8,32,128]{2,1,0:T(8,128)S(1)} %all_to_all.20.refs_0_, f32[1024,128]{1,0:T(8,128)S(1)} %get-tuple-element.10.refs_1_, f32[1024,128]{1,0:T(8,128)S(1)} %get-tuple-element.11.refs_2_, f32[16,8,128]{2,1,0:T(8,128)S(1)} %get-tuple-element.12.refs_3_, f32[1,3,3,512]{3,2,1,0:T(4,128)S(1)} %copy.12.refs_1_.refs_4_, ...), custom_call_target="tpu_custom_call" | custom-call | tf_op jit(solution)/shard_map/gate/pallas_call | solution.py:264
  77.8 30.6 %all_to_all.21.refs_0_ = bf16[8,512,128]{2,1,0:T(8,128)(2,1)S(1)} all-to-all(bf16[8,512,128]{2,1,0:T(8,128)(2,1)S(1)} %gate.1), channel_id=1, replica_groups={{0,16,32,48,2,18,34,50},{4,20,36,52,6,22,38,54},{8,24,40,56,10,26,42,58..., dimensions={0} | all-to-all | bytes 2097152 | tf_op jit(solution)/shard_map/all_to_all | solution.py:342
  108.4 0.0 all-gather.3.cloned.1.call-done
  108.4 0.0 copy-start
  108.4 1.6 %copy-done = bf16[16,512,128]{2,1,0:T(8,128)(2,1)S(1)} copy-done((bf16[16,512,128]{2,1,0:T(8,128)(2,1)S(1)}, bf16[16,512,128]{2,1,0:T(8,128)(2,1)}, u32[]{:S(2)}) %copy-start) | copy-done | bytes 2097176
  110.0 1.6 %product.1 = bf16[4,2,256,256]{3,2,1,0:T(8,128)(2,1)S(1)} custom-call(bf16[8,512,128]{2,1,0:T(8,128)(2,1)S(1)} %all_to_all.21.refs_0_, bf16[8,2,512,128]{3,2,1,0:T(8,128)(2,1)S(1)} %bitcast.7), custom_call_target="tpu_custom_call" | custom-call | tf_op jit(solution)/shard_map/product/pallas_call | solution.py:276
  111.6 0.0 copy-start.1
  111.6 0.0 copy-start.7
  111.7 14.3 %all_to_all.22.in_ref = bf16[8,256,256]{2,1,0:T(8,128)(2,1)S(1)} all-to-all(bf16[8,256,256]{2,1,0:T(8,128)(2,1)S(1)} %bitcast.6), channel_id=1, replica_groups={{0,16,4,20,8,24,12,28},{2,18,6,22,10,26,14,30},{32,48,36,52,40,56,44,60..., dimensions={0} | all-to-all | bytes 2097152 | tf_op jit(solution)/shard_map/all_to_all | solution.py:345
  125.9 0.0 copy-done.1
  126.0 0.0 copy-done.7
  126.0 1.7 %rotate.1 = bf16[256,512]{1,0:T(8,128)(2,1)S(1)} custom-call(bf16[8,256,256]{2,1,0:T(8,128)(2,1)S(1)} %all_to_all.22.in_ref, s32[1,512]{1,0:T(1,128)S(1)} %copy-done.7, bf16[512,512]{1,0:T(8,128)(2,1)S(1)} %copy-done.1), custom_call_target="tpu_custom_call" | custom-call | tf_op jit(solution)/shard_map/rotate/pallas_call | solution.py:293
  127.6 8.3 %collective-permute-start.2 = (bf16[256,512]{1,0:T(8,128)(2,1)S(1)}, bf16[256,512]{1,0:T(8,128)(2,1)S(1)}, u32[]{:S(2)}, u32[]{:S(2)}) collective-permute-start(bf16[256,512]{1,0:T(8,128)(2,1)S(1)} %rotate.1), channel_id=1, source_target_pairs={{0,1},{1,0},{2,3},{3,2},{4,5},{5,4},{6,7},{7,6},{8,9},{9,8},{10,11... | collective-permute-start | bytes 786440 | tf_op jit(solution)/shard_map/ppermute | solution.py:347
  136.0 1.1 collective-permute-done.2
  137.1 0.7 copy.15
  (1 shorter events, 0.0 us)
Async XLA Ops:
  6.5 23.1 %copy-start.8 = (f32[1,3,3,512]{3,0,2,1:T(1,128)S(1)}, f32[1,3,3,512]{3,0,2,1:T(1,128)}, u32[]{:S(2)}) copy-start(f32[1,3,3,512]{3,0,2,1:T(1,128)} %param.12) | copy-start | bytes 55300
  6.5 42.7 %copy-start.5 = (f32[1,16,512]{2,1,0:T(8,128)S(1)}, f32[1,16,512]{2,1,0:T(8,128)}, u32[]{:S(2)}) copy-start(f32[1,16,512]{2,1,0:T(8,128)} %refs_5_.1) | copy-start | bytes 98308
  6.5 101.9 %all-gather.3.cloned.1.call-start = ((), (), s32[]{:S(2)}) async-start(), calls=%async_computation.4 | async-start | bytes 2359296 | tf_op jit(solution)/shard_map/all_gather | solution.py:336
  6.5 6.7 %collective-permute-start = (bf16[512,128]{1,0:T(8,128)(2,1)}, bf16[512,128]{1,0:T(8,128)(2,1)S(1)}, u32[]{:S(2)}, u32[]{:S(2)}) collective-permute-start(bf16[512,128]{1,0:T(8,128)(2,1)} %bitcast.11), channel_id=1, source_target_pairs={{0,0},{2,64},{4,4},{6,68},{8,8},{10,72},{12,12},{14,76},{16,16},{1... | collective-permute-start | bytes 393224 | tf_op jit(solution)/shard_map/ppermute | solution.py:335
  8.2 10.4 %collective-permute-start.1 = (bf16[512,128]{1,0:T(8,128)(2,1)}, bf16[512,128]{1,0:T(8,128)(2,1)S(1)}, u32[]{:S(2)}, u32[]{:S(2)}) collective-permute-start(bf16[512,128]{1,0:T(8,128)(2,1)} %bitcast.12), channel_id=1, source_target_pairs={{0,32},{2,96},{4,36},{6,100},{8,40},{10,104},{12,44},{14,108},{16,... | collective-permute-start | bytes 393224 | tf_op jit(solution)/shard_map/ppermute | solution.py:335
  19.4 1.0 copy-start.2
  20.3 0.9 copy-start.3
  21.3 0.9 copy-start.4
  22.2 53.0 %copy-start.6 = (f32[1,16,512]{2,1,0:T(8,128)S(1)}, f32[1,16,512]{2,1,0:T(8,128)}, u32[]{:S(2)}) copy-start(f32[1,16,512]{2,1,0:T(8,128)} %refs_6_.1) | copy-start | bytes 98308
  23.4 25.8 %all-to-all-start = ((bf16[4,3,256,128]{3,2,1,0:T(8,128)(2,1)}), bf16[4,3,256,128]{3,2,1,0:T(8,128)(2,1)S(1)}, u32[]{:S(2)}, u32[]{:S(2)}) async-start(bf16[4,3,256,128]{3,2,1,0:T(8,128)(2,1)} %spread.1), calls=%async_computation | async-start | bytes 1572864 | tf_op jit(solution)/shard_map/all_to_all | solution.py:338
  108.4 1.6 %copy-start = (bf16[16,512,128]{2,1,0:T(8,128)(2,1)S(1)}, bf16[16,512,128]{2,1,0:T(8,128)(2,1)}, u32[]{:S(2)}) copy-start(bf16[16,512,128]{2,1,0:T(8,128)(2,1)} %all-gather.3.cloned.1.call-done) | copy-start | bytes 6291460
  111.6 14.3 %copy-start.1 = (bf16[512,512]{1,0:T(8,128)(2,1)S(1)}, bf16[512,512]{1,0:T(8,128)(2,1)}, u32[]{:S(2)}) copy-start(bf16[512,512]{1,0:T(8,128)(2,1)} %constant.2.clone.matrix_ref) | copy-start | bytes 1572868
  111.6 14.3 %copy-start.7 = (s32[1,512]{1,0:T(1,128)S(1)}, s32[1,512]{1,0:T(1,128)}, u32[]{:S(2)}) copy-start(s32[1,512]{1,0:T(1,128)} %sign_ref.1) | copy-start | bytes 6148
  127.6 9.5 %collective-permute-start.2 = (bf16[256,512]{1,0:T(8,128)(2,1)S(1)}, bf16[256,512]{1,0:T(8,128)(2,1)S(1)}, u32[]{:S(2)}, u32[]{:S(2)}) collective-permute-start(bf16[256,512]{1,0:T(8,128)(2,1)S(1)} %rotate.1), channel_id=1, source_target_pairs={{0,1},{1,0},{2,3},{3,2},{4,5},{5,4},{6,7},{7,6},{8,9},{9,8},{10,11... | collective-permute-start | bytes 786440 | tf_op jit(solution)/shard_map/ppermute | solution.py:347
Sparse Core Ops, SparseCore 0:
  19.5 55.0 all-gather.2
